TPU v7x, 512 devices: a whole 4x8x8 slice. The times are simulated.
512 devices in a mesh: rows: 128 (over y, z, core), cols: 4 (over x).
Axes of the slice: x: 4, y: 8, z: 8, core: 2. Of those that a mesh axis runs over, the one named last changes fastest.
Arguments:
- panel: float32 [16, 8388608], P('cols', 'rows')
- signs: int32 [8388608], P('rows'), may hold values from -1 to 1, as said below
- samples: int32 [65536], replicated, may hold values from 0 to 8388607, as said below
Outputs:
- factor: float32 [16, 16], replicated
- normalized: float32 [16, 114688], P('cols', 'rows')
Inputs may be any that keep to these rules, and one draw needn't show every extreme that they name: samples is strictly increasing. For every block d of positions, at most 896 samples g have (g mod 65536) // 512 == d, and some block has exactly 896. `signs`: every entry is -1 or 1.
All inputs are finite; a program needn't handle non-finite values.
Results may differ from a plain program's by a relative error of at most 0.00016.
Values sent between devices are 32-bit elements; how exact they have to be, the bound alone decides.
A program may use at most 128 MiB of HBM per device.

v0:
```python
import math

import jax
import jax.numpy as jnp
from jax import lax
from jax.sharding import PartitionSpec as P

CAP = 896


def from_partner(shard, axis, bit):
    return lax.ppermute(shard, axis, [(i, i ^ 1 << bit) for i in range(lax.axis_size(axis))])


def hadamard(order):
    first = jnp.arange(order, dtype=jnp.int32)
    both = jnp.bitwise_and(first[:, None], first[None, :])
    parity = jnp.zeros((order, order), jnp.int32)
    for level in range(max(order.bit_length() - 1, 0)):
        parity = parity + jnp.bitwise_and(jnp.right_shift(both, level), 1)
    parity = parity % 2
    return (1 - 2 * parity).astype(jnp.float32)


def local_transform(values):
    width, length = values.shape
    bits = length.bit_length() - 1
    outer = 1 << bits // 2
    inner = length // outer
    high = lax.Precision.HIGHEST
    shaped = values.reshape(width, outer, inner)
    shaped = jnp.einsum("cab,jb->caj", shaped, hadamard(inner), precision=high)
    shaped = jnp.einsum("ia,caj->cij", hadamard(outer), shaped, precision=high)
    return shaped.reshape(width, length)


def local(panel, signs, samples):
    width, local_rows = panel.shape
    row_devices = lax.axis_size("rows")
    block_rows = local_rows // row_devices
    total = local_rows * row_devices
    high = lax.Precision.HIGHEST
    my_index = lax.axis_index("rows")
    values = panel * signs[None, :].astype(jnp.float32) * (1.0 / math.sqrt(total))
    values = local_transform(values)
    for level in range(row_devices.bit_length() - 1):
        partner = from_partner(values, "rows", level)
        upper = my_index >> level & 1 == 1
        values = jnp.where(upper, partner - values, values + partner)
    shaped = values.reshape(width, row_devices, block_rows)
    shaped = lax.all_to_all(shaped, "rows", split_axis=1, concat_axis=1, tiled=True)
    flat = shaped.reshape(width, local_rows)
    sample_total = samples.shape[0]
    shard_ids = jnp.arange(row_devices, dtype=jnp.int32)
    base_rows = shard_ids * local_rows + my_index * block_rows
    lower_edges = jnp.searchsorted(samples, base_rows, side="left")
    upper_edges = jnp.searchsorted(samples, base_rows + block_rows, side="left")
    shard_counts = upper_edges - lower_edges
    block_ends = jnp.cumsum(shard_counts)
    block_starts = block_ends - shard_counts
    slot_ids = jnp.arange(CAP, dtype=jnp.int32)
    owner_shard = jnp.sum((slot_ids[:, None] >= block_ends[None, :]).astype(jnp.int32), axis=1)
    owner_shard = jnp.minimum(owner_shard, row_devices - 1)
    one_hot = (owner_shard[:, None] == shard_ids[None, :]).astype(jnp.int32)
    slot_lower = jnp.sum(one_hot * lower_edges[None, :], axis=1)
    slot_start = jnp.sum(one_hot * block_starts[None, :], axis=1)
    valid = slot_ids < block_ends[row_devices - 1]
    sample_pos = jnp.clip(slot_lower + slot_ids - slot_start, 0, sample_total - 1)
    chosen = samples[sample_pos]
    position = chosen // local_rows * block_rows + chosen % local_rows - my_index * block_rows
    position = jnp.clip(position, 0, local_rows - 1)
    slot_values = jnp.where(valid[None, :], jnp.take(flat, position, axis=1), 0.0)
    everyone = lax.all_gather(slot_values, "cols", axis=0, tiled=True)
    gram = lax.psum(jnp.dot(everyone, everyone.T, precision=high), "rows")
    gram = gram / sample_total
    lower = jnp.linalg.cholesky(gram)
    solved = jax.scipy.linalg.solve_triangular(lower, everyone, lower=True)
    column_index = lax.axis_index("cols")
    own_columns = lax.dynamic_slice_in_dim(solved, column_index * width, width, 0)
    return (lower.T, own_columns)


def solution(mesh):
    return jax.shard_map(
        local,
        mesh=mesh,
        in_specs=(P("cols", "rows"), P("rows"), P()),
        out_specs=(P(), P("cols", "rows")),
        check_vma=False,
    )
```

profile of v0, /device:TPU:1, one launch (start us, length us, event | category | flops | bytes accessed | tf_op | source)
XLA Modules:
  0.0 626.3 jit_solution(2625800337127074119)
XLA Ops:
  7.1 8.8 %collective-permute-start = (f32[4,65536]{1,0:T(4,128)S(1)}, f32[4,65536]{1,0:T(4,128)S(1)}, u32[]{:S(2)}, u32[]{:S(2)}) collective-permute-start(f32[4,65536]{1,0:T(4,128)S(1)} %bitcast.37), channel_id=1, source_target_pairs={{0,4},{4,0},{8,12},{12,8},{16,20},{20,16},{24,28},{28,24},{32,36},... | collective-permute-start | bytes 3145736 | tf_op jit(solution)/shard_map/ppermute | solution.py:12
  15.9 2.3 collective-permute-done
  18.4 1.9 collective-permute-start.1
  20.3 24.3 %collective-permute-done.1 = f32[4,65536]{1,0:T(4,128)S(1)} collective-permute-done((f32[4,65536]{1,0:T(4,128)S(1)}, f32[4,65536]{1,0:T(4,128)S(1)}, u32[]{:S(2)}, u32[]{:S(2)}) %collective-permute-start.1) | collective-permute-done | bytes 1048608 | tf_op jit(solution)/shard_map/ppermute | solution.py:12
  44.9 1.9 collective-permute-start.2
  46.9 48.4 %collective-permute-done.2 = f32[4,65536]{1,0:T(4,128)S(1)} collective-permute-done((f32[4,65536]{1,0:T(4,128)S(1)}, f32[4,65536]{1,0:T(4,128)S(1)}, u32[]{:S(2)}, u32[]{:S(2)}) %collective-permute-start.2) | collective-permute-done | bytes 1048608 | tf_op jit(solution)/shard_map/ppermute | solution.py:12
  95.5 4.3 collective-permute-start.3
  99.9 48.3 %collective-permute-done.3 = f32[4,65536]{1,0:T(4,128)S(1)} collective-permute-done((f32[4,65536]{1,0:T(4,128)S(1)}, f32[4,65536]{1,0:T(4,128)S(1)}, u32[]{:S(2)}, u32[]{:S(2)}) %collective-permute-start.3) | collective-permute-done | bytes 1048608 | tf_op jit(solution)/shard_map/ppermute | solution.py:12
  148.5 1.9 collective-permute-start.4
  150.4 24.2 %collective-permute-done.4 = f32[4,65536]{1,0:T(4,128)S(1)} collective-permute-done((f32[4,65536]{1,0:T(4,128)S(1)}, f32[4,65536]{1,0:T(4,128)S(1)}, u32[]{:S(2)}, u32[]{:S(2)}) %collective-permute-start.4) | collective-permute-done | bytes 1048608 | tf_op jit(solution)/shard_map/ppermute | solution.py:12
  174.9 1.9 collective-permute-start.5
  176.8 48.3 %collective-permute-done.5 = f32[4,65536]{1,0:T(4,128)S(1)} collective-permute-done((f32[4,65536]{1,0:T(4,128)S(1)}, f32[4,65536]{1,0:T(4,128)S(1)}, u32[]{:S(2)}, u32[]{:S(2)}) %collective-permute-start.5) | collective-permute-done | bytes 1048608 | tf_op jit(solution)/shard_map/ppermute | solution.py:12
  225.4 2.2 collective-permute-start.6
  227.6 33.0 %while.38 = (s32[]{:T(128)}, u32[128]{0:T(128)S(1)}, u32[128]{0:T(128)S(1)}, s32[65536]{0:T(1024)}, s32[]{:T(128)}, /*index=5*/s32[]{:T(128)}, s32[]{:T(128)}, s32[]{}) while((s32[]{:T(128)}, u32[128]{0:T(128)S(1)}, u32[128]{0:T(128)S(1)}, s32[65536]{0:T(1024)}, s32[]{:T(128)}, /*index=5*/s32[]{:T(128)}, s32[]{:T(128)}, s32[]{}) %tuple.71), condition=%wide.region_3.4_spmd.clone, body=%wide.region_2.3_spmd.clone.sunk | while | flops 2948 | bytes 10352 | solution.py:56
  227.6 1.9 gather_fusion.1
  229.6 1.9 gather_fusion.1
  231.5 1.9 gather_fusion.1
  233.5 1.9 gather_fusion.1
  235.4 1.9 gather_fusion.1
  237.3 1.9 gather_fusion.1
  239.3 1.9 gather_fusion.1
  241.2 1.9 gather_fusion.1
  243.2 1.9 gather_fusion.1
  247.0 1.9 gather_fusion.1
  249.0 1.9 gather_fusion.1
  252.9 1.9 gather_fusion.1
  256.7 1.9 gather_fusion.1
  258.7 1.9 gather_fusion.1
  260.6 14.9 %collective-permute-done.6 = f32[4,65536]{1,0:T(4,128)S(1)} collective-permute-done((f32[4,65536]{1,0:T(4,128)S(1)}, f32[4,65536]{1,0:T(4,128)S(1)}, u32[]{:S(2)}, u32[]{:S(2)}) %collective-permute-start.6) | collective-permute-done | bytes 1048608 | tf_op jit(solution)/shard_map/ppermute | solution.py:12
  276.7 10.3 %all-to-all-start = ((f32[4,128,512]{2,0,1:T(4,128)}), f32[4,128,512]{2,0,1:T(4,128)S(1)}, u32[]{:S(2)}, u32[]{:S(2)}) async-start(f32[4,128,512]{2,0,1:T(4,128)} %bitcast.4), calls=%async_computation | async-start | bytes 2097152 | tf_op jit(solution)/shard_map/all_to_all | solution.py:51
  287.1 33.0 %while.37 = (s32[]{:T(128)}, u32[128]{0:T(128)S(1)}, u32[128]{0:T(128)S(1)}, s32[65536]{0:T(1024)}, s32[]{:T(128)}, /*index=5*/s32[]{:T(128)}, s32[]{:T(128)}, s32[]{}) while((s32[]{:T(128)}, u32[128]{0:T(128)S(1)}, u32[128]{0:T(128)S(1)}, s32[65536]{0:T(1024)}, s32[]{:T(128)}, /*index=5*/s32[]{:T(128)}, s32[]{:T(128)}, s32[]{}) %tuple.77), condition=%wide.region_1.2_spmd.clone, body=%wide.region_0.1_spmd.clone.sunk | while | flops 3076 | bytes 10352 | solution.py:57
  287.1 1.9 gather_fusion
  289.0 1.9 gather_fusion
  291.0 1.9 gather_fusion
  292.9 1.9 gather_fusion
  294.9 1.9 gather_fusion
  296.8 1.9 gather_fusion
  300.7 1.9 gather_fusion
  302.6 1.9 gather_fusion
  306.5 1.9 gather_fusion
  308.4 1.9 gather_fusion
  312.3 1.9 gather_fusion
  314.3 1.9 gather_fusion
  321.7 5.8 gather_fusion.2
  328.2 15.6 %copy.29 = f32[4,128,512]{0,2,1:T(8,128)} copy(f32[4,128,512]{2,0,1:T(4,128)S(1)} %all-to-all-done) | data formatting | bytes 2097152 | tf_op jit(solution)/shard_map/all_to_all | solution.py:51
  343.9 12.4 %gather_fusion.3 = f32[896,4]{1,0:T(8,128)S(1)} fusion(f32[4,65536]{0,1:T(8,128)} %bitcast.36, s32[1024]{0:T(1024)S(1)} %pad_clamp_fusion.2), kind=kCustom, calls=%fused_computation.3 | custom fusion | bytes 32256 | tf_op jit(solution)/shard_map/jit(_take)/gather | solution.py:72
  356.8 9.7 %all-gather = f32[4,4,896]{2,1,0:T(4,128)S(1)} all-gather(f32[1,4,896]{2,1,0:T(4,128)S(1)} %copy.30), channel_id=1, replica_groups=mesh['rows'=128,'cols'=4] {'cols'}, dimensions={0}, use_global_device_ids=true | all-gather | bytes 71680 | tf_op jit(solution)/shard_map/all_gather | solution.py:73
  366.7 254.0 %psum.7 = f32[16,16]{0,1:T(8,128)S(1)} all-reduce(f32[16,16]{0,1:T(8,128)S(1)} %fusion.67), channel_id=1, replica_groups=mesh['rows'=128,'cols'=4] {'rows'}, use_global_device_ids=true, to_apply=%region_8.9 | all-reduce | flops 256 | bytes 2048 | tf_op jit(solution)/shard_map/psum | solution.py:74
  (158 shorter events, 33.9 us)
Async XLA Ops:
  7.1 11.1 %collective-permute-start = (f32[4,65536]{1,0:T(4,128)S(1)}, f32[4,65536]{1,0:T(4,128)S(1)}, u32[]{:S(2)}, u32[]{:S(2)}) collective-permute-start(f32[4,65536]{1,0:T(4,128)S(1)} %bitcast.37), channel_id=1, source_target_pairs={{0,4},{4,0},{8,12},{12,8},{16,20},{20,16},{24,28},{28,24},{32,36},... | collective-permute-start | bytes 3145736 | tf_op jit(solution)/shard_map/ppermute | solution.py:12
  18.4 26.3 %collective-permute-start.1 = (f32[4,65536]{1,0:T(4,128)S(1)}, f32[4,65536]{1,0:T(4,128)S(1)}, u32[]{:S(2)}, u32[]{:S(2)}) collective-permute-start(f32[4,65536]{1,0:T(4,128)S(1)} %add_select_fusion.6), channel_id=1, source_target_pairs={{0,8},{4,12},{8,0},{12,4},{16,24},{20,28},{24,16},{28,20},{32,40},... | collective-permute-start | bytes 3145736 | tf_op jit(solution)/shard_map/ppermute | solution.py:12
  44.9 50.3 %collective-permute-start.2 = (f32[4,65536]{1,0:T(4,128)S(1)}, f32[4,65536]{1,0:T(4,128)S(1)}, u32[]{:S(2)}, u32[]{:S(2)}) collective-permute-start(f32[4,65536]{1,0:T(4,128)S(1)} %add_select_fusion.5), channel_id=1, source_target_pairs={{0,16},{4,20},{8,24},{12,28},{16,0},{20,4},{24,8},{28,12},{32,48},... | collective-permute-start | bytes 3145736 | tf_op jit(solution)/shard_map/ppermute | solution.py:12
  95.5 52.7 %collective-permute-start.3 = (f32[4,65536]{1,0:T(4,128)S(1)}, f32[4,65536]{1,0:T(4,128)S(1)}, u32[]{:S(2)}, u32[]{:S(2)}) collective-permute-start(f32[4,65536]{1,0:T(4,128)S(1)} %add_select_fusion.4), channel_id=1, source_target_pairs={{0,32},{4,36},{8,40},{12,44},{16,48},{20,52},{24,56},{28,60},{32,0... | collective-permute-start | bytes 3145736 | tf_op jit(solution)/shard_map/ppermute | solution.py:12
  148.5 26.1 %collective-permute-start.4 = (f32[4,65536]{1,0:T(4,128)S(1)}, f32[4,65536]{1,0:T(4,128)S(1)}, u32[]{:S(2)}, u32[]{:S(2)}) collective-permute-start(f32[4,65536]{1,0:T(4,128)S(1)} %add_select_fusion.3), channel_id=1, source_target_pairs={{0,64},{4,68},{8,72},{12,76},{16,80},{20,84},{24,88},{28,92},{32,9... | collective-permute-start | bytes 3145736 | tf_op jit(solution)/shard_map/ppermute | solution.py:12
  174.9 50.3 %collective-permute-start.5 = (f32[4,65536]{1,0:T(4,128)S(1)}, f32[4,65536]{1,0:T(4,128)S(1)}, u32[]{:S(2)}, u32[]{:S(2)}) collective-permute-start(f32[4,65536]{1,0:T(4,128)S(1)} %add_select_fusion.2), channel_id=1, source_target_pairs={{0,128},{4,132},{8,136},{12,140},{16,144},{20,148},{24,152},{28,15... | collective-permute-start | bytes 3145736 | tf_op jit(solution)/shard_map/ppermute | solution.py:12
  225.4 50.0 %collective-permute-start.6 = (f32[4,65536]{1,0:T(4,128)S(1)}, f32[4,65536]{1,0:T(4,128)S(1)}, u32[]{:S(2)}, u32[]{:S(2)}) collective-permute-start(f32[4,65536]{1,0:T(4,128)S(1)} %add_select_fusion.1), channel_id=1, source_target_pairs={{0,256},{4,260},{8,264},{12,268},{16,272},{20,276},{24,280},{28,28... | collective-permute-start | bytes 3145736 | tf_op jit(solution)/shard_map/ppermute | solution.py:12
  276.7 51.5 %all-to-all-start = ((f32[4,128,512]{2,0,1:T(4,128)}), f32[4,128,512]{2,0,1:T(4,128)S(1)}, u32[]{:S(2)}, u32[]{:S(2)}) async-start(f32[4,128,512]{2,0,1:T(4,128)} %bitcast.4), calls=%async_computation | async-start | bytes 2097152 | tf_op jit(solution)/shard_map/all_to_all | solution.py:51
where the time goes:
time: 629 us; the launch traced here: 626 us
  blocking collectives  264 us (42%)
  waiting for transfers between devices  211 us (34%)
  local copies, waits for them, and re-layouts  101 us (16%)
  starting transfers between devices  33.3 us (5%)
  other arithmetic  12.4 us (2%)
    psum x1, blocking collectives, local(): gram = lax.psum(jnp.dot(everyone, everyone.T, precision=high), 'rows')  254 us
    ppermute x7, waiting for transfers between devices, from_partner(): lax.ppermute(shard, axis, [(i, i ^ 1 << bit) for i in range(lax.axis_size...  211 us
    gather x34, local copies, waits for them, and re-layouts, local(): upper_edges = jnp.searchsorted(samples, base_rows + block_rows, side='left')  64 us
    ppermute x7, starting transfers between devices, from_partner(): lax.ppermute(shard, axis, [(i, i ^ 1 << bit) for i in range(lax.axis_size...  23 us
    all_to_all x1, local copies, waits for them, and re-layouts, local(): lax.all_to_all(shaped, 'rows', split_axis=1, concat_axis=1, tiled=True)  15.6 us
  transfers between devices with their start and end apart: 8, of which 7 were waited for; matrix products, arithmetic and copies ran while one was open for 12% of the time, Pallas kernels for 0%

commit v1 on v0

v1 whole, which is shorter than its diff:
```python
import math

import jax
import jax.numpy as jnp
from jax import lax
from jax.experimental import pallas as pl
from jax.experimental.pallas import tpu as pltpu
from jax.sharding import PartitionSpec as P

LINE = 8
BLK = 512
LANES = 128
SLOT_ROWS = 7
CAP = SLOT_ROWS * LANES
WIDTH = 4
ORDER = 256
SHARDS = 128
LOCAL = ORDER * ORDER
SAMPLE_ROWS = 512
COLS = 16
MESH = pl.DeviceIdType.MESH
HIGHEST = lax.Precision.HIGHEST
DISTANCES = (4, 3, 5, 2, 6, 1, 7)


def iota(shape, axis):
    return lax.broadcasted_iota(jnp.int32, shape, axis)


def parity(value):
    value = value ^ (value >> 4)
    value = value ^ (value >> 2)
    value = value ^ (value >> 1)
    return value & 1


def hadamard_rows(rows):
    odd = parity(rows & iota((ORDER, ORDER), 1))
    return (1 - 2 * odd).astype(jnp.float32).astype(jnp.bfloat16)


def line_rows(half):
    place = iota((ORDER, ORDER), 0)
    line, core, other, part = place >> 5, (place >> 4) & 1, (place >> 1) & 7, place & 1
    if half == 0:
        return other * 32 + line * 4 + core * 2 + part
    return line * 32 + other * 4 + core * 2 + part


def split(values):
    high = values.astype(jnp.bfloat16)
    low = (values - high.astype(jnp.float32)).astype(jnp.bfloat16)
    return high, low


def dot(a, b):
    return jnp.dot(a, b, preferred_element_type=jnp.float32)


def slot_list(samples, device):
    turned = jnp.transpose(samples)
    pieces = [turned & 255, (turned >> 8) & 255, turned >> 16]
    pieces = [p.astype(jnp.float32).astype(jnp.bfloat16) for p in pieces]
    last = samples[:, LANES - 1 :].astype(jnp.float32)
    lane = iota((1, 2 * SHARDS), 1)
    edge = (lane & (SHARDS - 1)) * LOCAL + device * BLK + (lane >> 7) * BLK
    edge = edge.astype(jnp.float32)
    before = jnp.sum((last < edge).astype(jnp.float32), axis=0, keepdims=True)
    row_id = iota((SAMPLE_ROWS, 1), 0).astype(jnp.float32)
    hot = (row_id == before).astype(jnp.float32).astype(jnp.bfloat16)
    rows = dot(jnp.concatenate(pieces, axis=0), hot)
    rows = rows[:LANES] + 256.0 * rows[LANES : 2 * LANES] + 65536.0 * rows[2 * LANES :]
    inside = jnp.sum((rows < edge).astype(jnp.float32), axis=0, keepdims=True)
    whole = jnp.float32(SAMPLE_ROWS * LANES)
    place = jnp.where(before >= SAMPLE_ROWS, whole, before * LANES + inside)
    first = place[:, :SHARDS]
    count = place[:, SHARDS:] - first
    square_row, square_col = iota((SHARDS, SHARDS), 0), iota((SHARDS, SHARDS), 1)
    first_col = jnp.sum(
        jnp.where(square_row == square_col, first, 0.0), axis=1, keepdims=True
    )
    start_col = jnp.sum(
        jnp.where(square_col < square_row, count, 0.0), axis=1, keepdims=True
    )
    end_col = jnp.sum(
        jnp.where(square_col <= square_row, count, 0.0), axis=1, keepdims=True
    )
    slot = iota((1, CAP), 1).astype(jnp.float32)
    owner = jnp.sum((slot >= end_col).astype(jnp.float32), axis=0, keepdims=True)
    shard_id = iota((SHARDS, 1), 0).astype(jnp.float32)
    shift = jnp.sum(
        jnp.where(shard_id == owner, first_col - start_col, 0.0), axis=0, keepdims=True
    )
    index = slot + shift
    row = jnp.floor(index * (1.0 / LANES))
    column = index - row * LANES
    hot = (row_id == row).astype(jnp.float32).astype(jnp.bfloat16)
    bit = ((turned >> 8) & 1).astype(jnp.float32).astype(jnp.bfloat16)
    found = dot(jnp.concatenate([pieces[0], bit], axis=0), hot)
    found = found[:LANES] + 256.0 * found[LANES:]
    lane_id = iota((LANES, 1), 0).astype(jnp.float32)
    position = jnp.sum(
        jnp.where(lane_id == column, found, 0.0), axis=0, keepdims=True
    )
    used = owner < SHARDS
    code = jnp.where(used, owner * BLK + position, 0.0)
    return code.astype(jnp.int32), used.astype(jnp.float32)


def kernel(
    panel,
    signs,
    samples,
    factor,
    normalized,
    panel_v,
    signs_v,
    samples_v,
    sent,
    got,
    own_list,
    own_used,
    lists,
    codes,
    sums,
    part_sent,
    part_got,
    picked,
    gram_one,
    gram_two,
    local_sem,
    sent_sem,
    got_sem,
    list_out_sem,
    list_in_sem,
    part_out_sem,
    part_in_sem,
    picked_out_sem,
    picked_in_sem,
    one_out_sem,
    one_in_sem,
    two_out_sem,
    two_in_sem,
):
    scale = 1.0 / math.sqrt(LOCAL * SHARDS)
    me = lax.axis_index("rows")
    my_col = lax.axis_index("cols")
    my_y, my_z, my_core = me >> 4, (me >> 1) & 7, me & 1
    my_lines = (my_z, my_y)

    def device(half, line, core):
        if half == 0:
            return (my_y * 16 + line * 2 + core, my_col)
        return (line * 16 + my_z * 2 + core, my_col)

    def on_line(half, distance):
        return (my_lines[half] + distance) & 7

    loads = [
        pltpu.make_async_copy(samples, samples_v, local_sem.at[0]),
        pltpu.make_async_copy(signs, signs_v, local_sem.at[1]),
        pltpu.make_async_copy(panel, panel_v, local_sem.at[2]),
    ]
    for load in loads:
        load.start()

    barrier = pltpu.get_barrier_semaphore()

    def greet(target):
        pl.semaphore_signal(barrier, inc=1, device_id=target, device_id_type=MESH)

    greet(device(0, my_z, 1 - my_core))
    for distance in DISTANCES:
        for half in range(2):
            for flip in range(2):
                greet(device(half, on_line(half, distance), my_core ^ flip))
    for step in range(1, 4):
        greet((me, (my_col + step) & 3))

    loads[0].wait()
    code, used = slot_list(samples_v[...], me)
    for t in range(SLOT_ROWS):
        own_list[t : t + 1, :] = code[:, t * LANES : (t + 1) * LANES]
        own_used[t : t + 1, :] = used[:, t * LANES : (t + 1) * LANES]
    own_list[SLOT_ROWS:, :] = jnp.zeros((1, LANES), jnp.int32)
    own_used[SLOT_ROWS:, :] = jnp.zeros((1, LANES), jnp.float32)

    inner = hadamard_rows(iota((ORDER, ORDER), 0))
    outer = []
    for half in range(2):
        matrix = hadamard_rows(line_rows(half))
        outer.append(jnp.concatenate([matrix, matrix], axis=1))

    loads[1].wait()
    loads[2].wait()
    pl.semaphore_wait(barrier, 32)

    list_copies = []
    for half in range(2):
        lists[half, my_lines[half]] = own_list[...]
        for distance in DISTANCES:
            line = on_line(half, distance)
            copy = pltpu.make_async_remote_copy(
                src_ref=own_list,
                dst_ref=lists.at[half, my_lines[half]],
                send_sem=list_out_sem.at[half, line],
                recv_sem=list_in_sem.at[half, my_lines[half]],
                device_id=device(half, line, my_core),
                device_id_type=MESH,
            )
            copy.start()
            list_copies.append(copy)

    flip_signs = jnp.concatenate(
        [signs_v[pl.ds(j, ORDER, stride=2), :] for j in range(2)], axis=1
    )
    flip_signs = flip_signs.astype(jnp.float32) * scale
    my_sources = [my_lines[half] * 2 + my_core for half in range(2)]

    def block_copy(half, column, line, core):
        target = line * 2 + core
        return pltpu.make_async_remote_copy(
            src_ref=sent.at[half, target, column],
            dst_ref=got.at[half, my_sources[half], column],
            send_sem=sent_sem.at[half, target, column],
            recv_sem=got_sem.at[half, my_sources[half], column],
            device_id=device(half, line, core),
            device_id_type=MESH,
        )

    for column in range(2):
        for half in range(2):
            which = half * 2 + column
            values = jnp.concatenate(
                [panel_v[pl.ds(4 * j + which, ORDER, stride=8), :] for j in range(2)],
                axis=1,
            )
            high, low = split(values * flip_signs)
            values = dot(jnp.concatenate([high, low], axis=0), inner)
            values = values[:ORDER] + values[ORDER:]
            high, low = split(values)
            values = dot(outer[half], jnp.concatenate([high, low], axis=0))
            sent[half, :, column] = values.reshape(16, 16, ORDER)
            for distance in DISTANCES:
                for flip in range(2):
                    block_copy(
                        half, column, on_line(half, distance), my_core ^ flip
                    ).start()
            block_copy(half, column, my_lines[half], 1 - my_core).start()

    spread = iota((8, LANES), 0) >> 1
    for half in range(2):
        for distance in DISTANCES:
            line = on_line(half, distance)
            pltpu.make_async_remote_copy(
                src_ref=own_list,
                dst_ref=lists.at[half, line],
                send_sem=list_out_sem.at[half, line],
                recv_sem=list_in_sem.at[half, line],
                device_id=device(half, line, my_core),
                device_id_type=MESH,
            ).wait_recv()
        flat = lists.at[half].reshape(64, LANES)
        for t in range(SLOT_ROWS):
            rows = flat[pl.ds(t, 8, stride=8), :]
            for group in range(2):
                codes[1 - half, group, t] = jnp.take_along_axis(
                    rows, spread + 4 * group, axis=0
                )

    odd_row = iota((8, LANES), 0) & 1

    def add_source(half, column, source, table, first):
        for group in range(2):
            left = table[group * 8 : group * 8 + 8, :LANES]
            right = table[group * 8 : group * 8 + 8, LANES:]
            for t in range(SLOT_ROWS):
                code = codes[half, group, t]
                lane = code & (LANES - 1)
                a = jnp.take_along_axis(left, lane, axis=1)
                b = jnp.take_along_axis(right, lane, axis=1)
                value = jnp.where((code & LANES) != 0, b, a)
                shard = code >> 9
                if half == 0:
                    bits = shard & source
                else:
                    bits = shard & ((source >> 1) * 16 + (source & 1))
                value = jnp.where(parity(bits) != 0, -value, value)
                if first:
                    sums[half, column, group, t] = value
                else:
                    sums[half, column, group, t] += value

    def part_copy(half, column, line):
        return pltpu.make_async_remote_copy(
            src_ref=part_sent.at[half, column, line],
            dst_ref=part_got.at[half, column, my_lines[half]],
            send_sem=part_out_sem.at[half, column, line],
            recv_sem=part_in_sem.at[half, column, my_lines[half]],
            device_id=device(half, line, my_core),
            device_id_type=MESH,
        )

    for column in range(2):
        for half in range(2):
            mine = my_sources[half]
            add_source(half, column, mine, sent.at[half, mine, column], True)

            def from_source(line, core, half=half, column=column):
                source = line * 2 + core
                pltpu.make_async_remote_copy(
                    src_ref=sent.at[half, source, column],
                    dst_ref=got.at[half, source, column],
                    send_sem=sent_sem.at[half, source, column],
                    recv_sem=got_sem.at[half, source, column],
                    device_id=device(half, line, core),
                    device_id_type=MESH,
                ).wait_recv()
                add_source(
                    half, column, source, got.at[half, source, column], False
                )

            from_source(my_lines[half], 1 - my_core)

            def body(step, carry, half=half, from_source=from_source):
                order = step >> 1
                away = (order + 1) >> 1
                distance = 4 + away * (1 - 2 * (order & 1))
                from_source(on_line(half, distance), my_core ^ (step & 1))
                return carry

            lax.fori_loop(0, 14, body, 0)

            other = 1 - half
            for group in range(2):
                for t in range(SLOT_ROWS):
                    code = codes[half, group, t]
                    value = sums[half, column, group, t]
                    value = jnp.where(((code >> 8) & 1) == odd_row, value, 0.0)
                    value = value + pltpu.roll(value, 7, 0)
                    for line in range(4):
                        part_sent[other, column, group * 4 + line, t : t + 1, :] = (
                            value[2 * line : 2 * line + 1]
                        )
            for line in range(8):
                part_sent[other, column, line, SLOT_ROWS:, :] = jnp.zeros(
                    (1, LANES), jnp.float32
                )
            for distance in DISTANCES:
                part_copy(other, column, on_line(other, distance)).start()

    own_code = own_list[...] >> 9
    own_mask = own_used[...]
    for column in range(2):
        for half in range(2):
            other = 1 - half
            line = my_lines[other]
            bits = own_code >> 1 if other == 0 else own_code >> 4

            def signed(line, value):
                return jnp.where(parity(bits & line & 7) != 0, -value, value)

            total = signed(line, part_sent[other, column, line])
            for distance in DISTANCES:
                line = on_line(other, distance)
                pltpu.make_async_remote_copy(
                    src_ref=part_sent.at[other, column, line],
                    dst_ref=part_got.at[other, column, line],
                    send_sem=part_out_sem.at[other, column, line],
                    recv_sem=part_in_sem.at[other, column, line],
                    device_id=device(other, line, my_core),
                    device_id_type=MESH,
                ).wait_recv()
                total += signed(line, part_got[other, column, line])
            which = half * 2 + column
            picked[my_col, which * 8 : which * 8 + 8, :] = total * own_mask

    for step in range(1, 4):
        pltpu.make_async_remote_copy(
            src_ref=picked.at[my_col],
            dst_ref=picked.at[my_col],
            send_sem=picked_out_sem.at[(my_col + step) & 3],
            recv_sem=picked_in_sem.at[my_col],
            device_id=(me, (my_col + step) & 3),
            device_id_type=MESH,
        ).start()
    for step in range(1, 4):
        source = (my_col + step) & 3
        pltpu.make_async_remote_copy(
            src_ref=picked.at[my_col],
            dst_ref=picked.at[source],
            send_sem=picked_out_sem.at[source],
            recv_sem=picked_in_sem.at[source],
            device_id=(me, source),
            device_id_type=MESH,
        ).wait_recv()
    flat = picked.reshape(COLS * 8, LANES)
    panel_rows = jnp.concatenate(
        [flat[pl.ds(t, COLS, stride=8), :] for t in range(SLOT_ROWS)], axis=1
    )

    wide = lax.dot_general(
        panel_rows,
        jnp.concatenate([panel_rows] * 8, axis=0),
        (((1,), (1,)), ((), ())),
        precision=HIGHEST,
        preferred_element_type=jnp.float32,
    )
    keep = (iota((COLS, LANES), 1) >> 4) == (iota((COLS, LANES), 0) & 7)
    wide = jnp.where(keep, wide, 0.0) * (1.0 / (SAMPLE_ROWS * LANES))
    mine = my_sources[0]
    gram_one[mine] = jnp.concatenate(
        [
            jnp.sum(wide[:8], axis=0, keepdims=True),
            jnp.sum(wide[8:], axis=0, keepdims=True),
        ],
        axis=0,
    )

    sources = [(my_z, 1 - my_core)]
    for distance in DISTANCES:
        for flip in range(2):
            sources.append((on_line(0, distance), my_core ^ flip))
    for line, core in sources:
        pltpu.make_async_remote_copy(
            src_ref=gram_one.at[mine],
            dst_ref=gram_one.at[mine],
            send_sem=one_out_sem.at[line * 2 + core],
            recv_sem=one_in_sem.at[mine],
            device_id=device(0, line, core),
            device_id_type=MESH,
        ).start()
    for line, core in sources:
        pltpu.make_async_remote_copy(
            src_ref=gram_one.at[mine],
            dst_ref=gram_one.at[line * 2 + core],
            send_sem=one_out_sem.at[line * 2 + core],
            recv_sem=one_in_sem.at[line * 2 + core],
            device_id=device(0, line, core),
            device_id_type=MESH,
        ).wait_recv()
    gram_two[my_y] = jnp.sum(gram_one[...], axis=0)
    for distance in DISTANCES:
        line = on_line(1, distance)
        pltpu.make_async_remote_copy(
            src_ref=gram_two.at[my_y],
            dst_ref=gram_two.at[my_y],
            send_sem=two_out_sem.at[line],
            recv_sem=two_in_sem.at[my_y],
            device_id=device(1, line, my_core),
            device_id_type=MESH,
        ).start()
    for distance in DISTANCES:
        line = on_line(1, distance)
        pltpu.make_async_remote_copy(
            src_ref=gram_two.at[my_y],
            dst_ref=gram_two.at[line],
            send_sem=two_out_sem.at[line],
            recv_sem=two_in_sem.at[line],
            device_id=device(1, line, my_core),
            device_id_type=MESH,
        ).wait_recv()
    gram = jnp.sum(gram_two[...], axis=0)

    row = iota((COLS, LANES), 0)
    lane = iota((COLS, LANES), 1)
    rows = jnp.concatenate(
        [jnp.broadcast_to(gram[i : i + 1], (8, LANES)) for i in range(2)], axis=0
    )
    rows = jnp.take_along_axis(rows, ((row & 7) * 16 + lane) & (LANES - 1), axis=1)
    unit = jnp.where(lane - COLS == row, 1.0, 0.0)
    both = jnp.where(lane < COLS, rows, unit)
    for j in range(COLS - 1):
        pivot_row = jnp.broadcast_to(both[j : j + 1], (COLS, LANES))
        pivot = jnp.take_along_axis(pivot_row, jnp.full_like(lane, j), axis=1)
        column = jnp.take_along_axis(both, jnp.full_like(lane, j), axis=1)
        column = jnp.where(row > j, column, 0.0)
        both = both - column * (pivot_row / pivot)
    pivots = jnp.take_along_axis(both, row, axis=1)
    both = both / jnp.sqrt(pivots)
    factor[...] = jnp.where(lane >= row, both, 0.0)[:, :COLS]

    pick_row = iota((8, COLS), 1) == iota((8, COLS), 0) + my_col * WIDTH
    own = jnp.dot(
        pick_row.astype(jnp.float32),
        both[:, COLS : 2 * COLS],
        precision=HIGHEST,
        preferred_element_type=jnp.float32,
    )
    own = jnp.dot(
        own, panel_rows, precision=HIGHEST, preferred_element_type=jnp.float32
    )
    normalized[...] = own[:WIDTH]

    for copy in list_copies:
        copy.wait_send()
    for column in range(2):
        for half in range(2):
            block_copy(half, column, my_lines[half], 1 - my_core).wait_send()
            for distance in DISTANCES:
                for flip in range(2):
                    block_copy(
                        half, column, on_line(half, distance), my_core ^ flip
                    ).wait_send()
                part_copy(half, column, on_line(half, distance)).wait_send()
    for step in range(1, 4):
        pltpu.make_async_remote_copy(
            src_ref=picked.at[my_col],
            dst_ref=picked.at[my_col],
            send_sem=picked_out_sem.at[(my_col + step) & 3],
            recv_sem=picked_in_sem.at[my_col],
            device_id=(me, (my_col + step) & 3),
            device_id_type=MESH,
        ).wait_send()
    for line, core in sources:
        pltpu.make_async_remote_copy(
            src_ref=gram_one.at[mine],
            dst_ref=gram_one.at[mine],
            send_sem=one_out_sem.at[line * 2 + core],
            recv_sem=one_in_sem.at[mine],
            device_id=device(0, line, core),
            device_id_type=MESH,
        ).wait_send()
    for distance in DISTANCES:
        line = on_line(1, distance)
        pltpu.make_async_remote_copy(
            src_ref=gram_two.at[my_y],
            dst_ref=gram_two.at[my_y],
            send_sem=two_out_sem.at[line],
            recv_sem=two_in_sem.at[my_y],
            device_id=device(1, line, my_core),
            device_id_type=MESH,
        ).wait_send()


def local(panel, signs, samples):
    panel = panel.reshape(WIDTH, 2 * ORDER, LANES).transpose(1, 0, 2)
    panel = panel.reshape(2 * ORDER * WIDTH, LANES)
    signs = signs.reshape(2 * ORDER, LANES)
    samples = samples.reshape(SAMPLE_ROWS, LANES)
    f32, i32, dma = jnp.float32, jnp.int32, pltpu.SemaphoreType.DMA
    factor, normalized = pl.pallas_call(
        kernel,
        out_shape=(
            jax.ShapeDtypeStruct((COLS, COLS), f32),
            jax.ShapeDtypeStruct((WIDTH, CAP), f32),
        ),
        in_specs=[pl.BlockSpec(memory_space=pl.ANY)] * 3,
        out_specs=[pl.BlockSpec(memory_space=pltpu.VMEM)] * 2,
        scratch_shapes=[
            pltpu.VMEM((2 * ORDER * WIDTH, LANES), f32),
            pltpu.VMEM((2 * ORDER, LANES), i32),
            pltpu.VMEM((SAMPLE_ROWS, LANES), i32),
            pltpu.VMEM((2, 16, 2, 16, ORDER), f32),
            pltpu.VMEM((2, 16, 2, 16, ORDER), f32),
            pltpu.VMEM((8, LANES), i32),
            pltpu.VMEM((8, LANES), f32),
            pltpu.VMEM((2, 8, 8, LANES), i32),
            pltpu.VMEM((2, 2, SLOT_ROWS, 8, LANES), i32),
            pltpu.VMEM((2, 2, 2, SLOT_ROWS, 8, LANES), f32),
            pltpu.VMEM((2, 2, 8, 8, LANES), f32),
            pltpu.VMEM((2, 2, 8, 8, LANES), f32),
            pltpu.VMEM((4, 8 * WIDTH, LANES), f32),
            pltpu.VMEM((16, 2, LANES), f32),
            pltpu.VMEM((8, 2, LANES), f32),
            dma((3,)),
            dma((2, 16, 2)),
            dma((2, 16, 2)),
            dma((2, 8)),
            dma((2, 8)),
            dma((2, 2, 8)),
            dma((2, 2, 8)),
            dma((4,)),
            dma((4,)),
            dma((16,)),
            dma((16,)),
            dma((8,)),
            dma((8,)),
        ],
        compiler_params=pltpu.CompilerParams(
            collective_id=0, has_side_effects=True, vmem_limit_bytes=32 * 1024 * 1024
        ),
    )(panel, signs, samples)
    return factor, normalized


def solution(mesh):
    return jax.shard_map(
        local,
        mesh=mesh,
        in_specs=(P("cols", "rows"), P("rows"), P()),
        out_specs=(P(), P("cols", "rows")),
        check_vma=False,
    )
```

time: 629 us -> 59.8 us (0.10)
  blocking collectives: 264 us -> 0 us
  waiting for transfers between devices: 211 us -> 0 us
  local copies, waits for them, and re-layouts: 101 us -> 4.32 us
  Pallas kernels: 0 us -> 54.6 us
  starting transfers between devices: 33.3 us -> 0 us
  other arithmetic: 12.4 us -> 0 us
    psum x1 -> x0, blocking collectives: 254 us -> none  [local(): gram = lax.psum(jnp.dot(everyone, everyone.T, precision=high), 'rows')]
    ppermute x7 -> x0, waiting for transfers between devices: 211 us -> none  [from_partner(): lax.ppermute(shard, axis, [(i, i ^ 1 << bit) for i in range(lax.axis_size...]
    gather x36 -> x0, local copies, waits for them, and re-layouts: 82.2 us -> none  [the longest x34 64 us: local(): upper_edges = jnp.searchsorted(samples, base_rows + block_rows, side='left')]
    pallas_call x0 -> x1, Pallas kernels: none -> 54.6 us  [local(): pl.pallas_call(kernel, out_shape=(jax.ShapeDtypeStruct((COLS, COLS), f32)...]
    ppermute x7 -> x0, starting transfers between devices: 23 us -> none  [from_partner(): lax.ppermute(shard, axis, [(i, i ^ 1 << bit) for i in range(lax.axis_size...]
    all_to_all x1 -> x0, local copies, waits for them, and re-layouts: 15.6 us -> none  [local(): lax.all_to_all(shaped, 'rows', split_axis=1, concat_axis=1, tiled=True)]
    all_to_all x1 -> x0, starting transfers between devices: 10.3 us -> none  [local(): lax.all_to_all(shaped, 'rows', split_axis=1, concat_axis=1, tiled=True)]
    all_gather x1 -> x0, blocking collectives: 9.65 us -> none  [local(): everyone = lax.all_gather(slot_values, 'cols', axis=0, tiled=True)]
  transfers between devices with their start and end apart: 8 -> 0, of which waited for: 7 -> 0; matrix products, arithmetic and copies ran while one was open for 12% -> 0% of each run, Pallas kernels for 0% -> 0%
where the time goes in v1:
time: 59.8 us; the launch traced here: 59.5 us
  Pallas kernels  54.6 us (91%)
  local copies, waits for them, and re-layouts  4.32 us (7%)
  between operations  0.65 us (1%)
    pallas_call x1, Pallas kernels, local(): pl.pallas_call(kernel, out_shape=(jax.ShapeDtypeStruct((COLS, COLS), f32)...  54.6 us
    unnamed x8, local copies, waits for them, and re-layouts  4.32 us

profile of v1, /device:TPU:1, one launch (start us, length us, event | category | flops | bytes accessed | tf_op | source)
XLA Modules:
  0.0 59.5 jit_solution(2837676495497193890)
XLA Ops:
  0.6 0.0 copy-start
  0.6 1.2 %copy-done = f32[4,65536]{1,0:T(4,128)S(1)} copy-done((f32[4,65536]{1,0:T(4,128)S(1)}, f32[4,65536]{1,0:T(4,128)}, u32[]{:S(2)}) %copy-start) | copy-done | bytes 1048600
  1.9 0.0 copy-start.1
  1.9 0.9 %copy-done.1 = s32[65536]{0:T(1024)S(1)} copy-done((s32[65536]{0:T(1024)S(1)}, s32[65536]{0:T(1024)}, u32[]{:S(2)}) %copy-start.1) | copy-done | bytes 262168
  2.8 0.0 copy-start.2
  2.8 0.9 %copy-done.2 = s32[65536]{0:T(1024)S(1)} copy-done((s32[65536]{0:T(1024)S(1)}, s32[65536]{0:T(1024)}, u32[]{:S(2)}) %copy-start.2) | copy-done | bytes 262168
  3.8 54.6 %shard_map.50 = (f32[16,16]{1,0:T(8,128)S(1)}, f32[4,896]{1,0:T(4,128)S(1)}) custom-call(f32[2048,128]{1,0:T(8,128)S(1)} %bitcast.7, s32[512,128]{1,0:T(8,128)S(1)} %bitcast.8, s32[512,128]{1,0:T(8,128)S(1)} %bitcast.9), custom_call_target="tpu_custom_call" | custom-call | tf_op jit(solution)/shard_map/pallas_call | solution.py:542
  58.3 0.6 %copy.8 = f32[16,16]{1,0:T(8,128)} copy(f32[16,16]{1,0:T(8,128)S(1)} %get-tuple-element.4) | data formatting | bytes 2048
  58.9 0.6 %copy.9 = f32[4,896]{1,0:T(4,128)} copy(f32[4,896]{1,0:T(4,128)S(1)} %get-tuple-element.5) | data formatting | bytes 28672
Async XLA Ops:
  0.6 1.2 %copy-start = (f32[4,65536]{1,0:T(4,128)S(1)}, f32[4,65536]{1,0:T(4,128)}, u32[]{:S(2)}) copy-start(f32[4,65536]{1,0:T(4,128)} %param.3) | copy-start | bytes 3145732
  1.9 0.9 %copy-start.1 = (s32[65536]{0:T(1024)S(1)}, s32[65536]{0:T(1024)}, u32[]{:S(2)}) copy-start(s32[65536]{0:T(1024)} %param.4) | copy-start | bytes 786436
  2.8 0.9 %copy-start.2 = (s32[65536]{0:T(1024)S(1)}, s32[65536]{0:T(1024)}, u32[]{:S(2)}) copy-start(s32[65536]{0:T(1024)} %param.5) | copy-start | bytes 786436

commit v2 on v0

v2 whole, which is shorter than its diff:
```python
import math

import jax
import jax.numpy as jnp
from jax import lax
from jax.experimental import pallas as pl
from jax.experimental.pallas import tpu as pltpu
from jax.sharding import PartitionSpec as P

LINE = 8
BLK = 512
LANES = 128
SLOT_ROWS = 7
CAP = SLOT_ROWS * LANES
WIDTH = 4
ORDER = 256
SHARDS = 128
LOCAL = ORDER * ORDER
SAMPLE_ROWS = 512
COLS = 16
MESH = pl.DeviceIdType.MESH
HIGHEST = lax.Precision.HIGHEST
DISTANCES = (4, 3, 5, 2, 6, 1, 7)
OFFSETS = sorted(
    ((y, z, c) for y in range(8) for z in range(8) for c in range(2) if y or z or c),
    key=lambda at: -min(at[0], 8 - at[0]) - min(at[1], 8 - at[1]),
)


def iota(shape, axis):
    return lax.broadcasted_iota(jnp.int32, shape, axis)


def parity(value):
    value = value ^ (value >> 4)
    value = value ^ (value >> 2)
    value = value ^ (value >> 1)
    return value & 1


def hadamard_rows(rows):
    odd = parity(rows & iota((ORDER, ORDER), 1))
    return (1 - 2 * odd).astype(jnp.float32).astype(jnp.bfloat16)


def line_rows(half):
    place = iota((ORDER, ORDER), 0)
    line, core, other, part = place >> 5, (place >> 4) & 1, (place >> 1) & 7, place & 1
    if half == 0:
        return other * 32 + line * 4 + core * 2 + part
    return line * 32 + other * 4 + core * 2 + part


def split(values):
    high = values.astype(jnp.bfloat16)
    low = (values - high.astype(jnp.float32)).astype(jnp.bfloat16)
    return high, low


def dot(a, b):
    return jnp.dot(a, b, preferred_element_type=jnp.float32)


def slot_list(samples, device):
    turned = jnp.transpose(samples)
    pieces = [turned & 255, (turned >> 8) & 255, turned >> 16]
    pieces = [p.astype(jnp.float32).astype(jnp.bfloat16) for p in pieces]
    last = samples[:, LANES - 1 :].astype(jnp.float32)
    lane = iota((1, 2 * SHARDS), 1)
    edge = (lane & (SHARDS - 1)) * LOCAL + device * BLK + (lane >> 7) * BLK
    edge = edge.astype(jnp.float32)
    before = jnp.sum((last < edge).astype(jnp.float32), axis=0, keepdims=True)
    row_id = iota((SAMPLE_ROWS, 1), 0).astype(jnp.float32)
    hot = (row_id == before).astype(jnp.float32).astype(jnp.bfloat16)
    rows = dot(jnp.concatenate(pieces, axis=0), hot)
    rows = rows[:LANES] + 256.0 * rows[LANES : 2 * LANES] + 65536.0 * rows[2 * LANES :]
    inside = jnp.sum((rows < edge).astype(jnp.float32), axis=0, keepdims=True)
    whole = jnp.float32(SAMPLE_ROWS * LANES)
    place = jnp.where(before >= SAMPLE_ROWS, whole, before * LANES + inside)
    first = place[:, :SHARDS]
    count = place[:, SHARDS:] - first
    square_row, square_col = iota((SHARDS, SHARDS), 0), iota((SHARDS, SHARDS), 1)
    first_col = jnp.sum(
        jnp.where(square_row == square_col, first, 0.0), axis=1, keepdims=True
    )
    start_col = jnp.sum(
        jnp.where(square_col < square_row, count, 0.0), axis=1, keepdims=True
    )
    end_col = jnp.sum(
        jnp.where(square_col <= square_row, count, 0.0), axis=1, keepdims=True
    )
    slot = iota((1, CAP), 1).astype(jnp.float32)
    owner = jnp.sum((slot >= end_col).astype(jnp.float32), axis=0, keepdims=True)
    shard_id = iota((SHARDS, 1), 0).astype(jnp.float32)
    shift = jnp.sum(
        jnp.where(shard_id == owner, first_col - start_col, 0.0), axis=0, keepdims=True
    )
    index = slot + shift
    row = jnp.floor(index * (1.0 / LANES))
    column = index - row * LANES
    hot = (row_id == row).astype(jnp.float32).astype(jnp.bfloat16)
    bit = ((turned >> 8) & 1).astype(jnp.float32).astype(jnp.bfloat16)
    found = dot(jnp.concatenate([pieces[0], bit], axis=0), hot)
    found = found[:LANES] + 256.0 * found[LANES:]
    lane_id = iota((LANES, 1), 0).astype(jnp.float32)
    position = jnp.sum(
        jnp.where(lane_id == column, found, 0.0), axis=0, keepdims=True
    )
    used = owner < SHARDS
    code = jnp.where(used, owner * BLK + position, 0.0)
    return code.astype(jnp.int32), used.astype(jnp.float32)


def kernel(
    panel,
    signs,
    samples,
    factor,
    normalized,
    panel_v,
    signs_v,
    samples_v,
    sent,
    got,
    own_list,
    own_used,
    lists,
    codes,
    part_sent,
    part_got,
    picked,
    grams,
    local_sem,
    out_sem,
    list_sem,
    block_sem,
    part_sem,
    picked_sem,
    gram_sem,
):
    scale = 1.0 / math.sqrt(LOCAL * SHARDS)
    me = lax.axis_index("rows")
    my_col = lax.axis_index("cols")
    my_y, my_z, my_core = me >> 4, (me >> 1) & 7, me & 1
    my_lines = (my_z, my_y)
    my_sources = [my_lines[half] * 2 + my_core for half in range(2)]

    def device(half, line, core):
        if half == 0:
            return (my_y * 16 + line * 2 + core, my_col)
        return (line * 16 + my_z * 2 + core, my_col)

    def on_line(half, distance):
        return (my_lines[half] + distance) & 7

    def send(src, dst, out, arrived, target):
        pltpu.make_async_remote_copy(
            src_ref=src,
            dst_ref=dst,
            send_sem=out_sem.at[out],
            recv_sem=arrived,
            device_id=target,
            device_id_type=MESH,
        ).start()

    def wait_arrived(like, arrived):
        pltpu.make_async_copy(like, like, arrived).wait()

    def wait_left(like, out):
        pltpu.make_async_copy(like, like, out_sem.at[out]).wait()

    loads = [
        pltpu.make_async_copy(panel, panel_v, local_sem.at[2]),
        pltpu.make_async_copy(signs, signs_v, local_sem.at[1]),
        pltpu.make_async_copy(samples, samples_v, local_sem.at[0]),
    ]
    for load in loads:
        load.start()

    barrier = pltpu.get_barrier_semaphore()

    def greet(target):
        pl.semaphore_signal(barrier, inc=1, device_id=target, device_id_type=MESH)

    for distance in DISTANCES:
        for half in range(2):
            for flip in range(2):
                greet(device(half, on_line(half, distance), my_core ^ flip))
    for step in range(1, 4):
        greet((me, (my_col + step) & 3))
    greet(device(0, my_z, 1 - my_core))

    inner = hadamard_rows(iota((ORDER, ORDER), 0))
    outer = []
    for half in range(2):
        matrix = hadamard_rows(line_rows(half))
        outer.append(jnp.concatenate([matrix, matrix], axis=1))

    loads[1].wait()
    loads[0].wait()
    flip_signs = jnp.concatenate(
        [signs_v[pl.ds(j, ORDER, stride=2), :] for j in range(2)], axis=1
    )
    flip_signs = flip_signs.astype(jnp.float32) * scale

    def transform(pair):
        half = pair & 1
        values = jnp.concatenate(
            [panel_v[pl.ds(4 * j + pair, ORDER, stride=8), :] for j in range(2)],
            axis=1,
        )
        high, low = split(values * flip_signs)
        values = dot(jnp.concatenate([high, low], axis=0), inner)
        values = values[:ORDER] + values[ORDER:]
        high, low = split(values)
        values = dot(outer[half], jnp.concatenate([high, low], axis=0))
        sent[pair] = values.reshape(16, 16, ORDER)
        got[pair, my_sources[half]] = sent[pair, my_sources[half]]

    def send_block(pair, half, line, core):
        send(
            sent.at[pair, line * 2 + core],
            got.at[pair, my_sources[half]],
            1,
            block_sem.at[pair],
            device(half, line, core),
        )

    def send_blocks(first):
        for distance in DISTANCES:
            for half in range(2):
                for flip in range(2):
                    send_block(
                        first + half, half, on_line(half, distance), my_core ^ flip
                    )
        for half in range(2):
            send_block(first + half, half, my_lines[half], 1 - my_core)

    transform(0)
    transform(1)
    pl.semaphore_wait(barrier, 32)
    send_blocks(0)
    transform(2)
    transform(3)

    loads[2].wait()
    code, used = slot_list(samples_v[...], me)
    for t in range(SLOT_ROWS):
        own_list[t : t + 1, :] = code[:, t * LANES : (t + 1) * LANES]
        own_used[t : t + 1, :] = used[:, t * LANES : (t + 1) * LANES]
    own_list[SLOT_ROWS:, :] = jnp.zeros((1, LANES), jnp.int32)
    own_used[SLOT_ROWS:, :] = jnp.zeros((1, LANES), jnp.float32)
    for half in range(2):
        lists[half, my_lines[half]] = own_list[...]
        for distance in DISTANCES:
            line = on_line(half, distance)
            send(
                own_list,
                lists.at[half, my_lines[half]],
                0,
                list_sem.at[half],
                device(half, line, my_core),
            )
    send_blocks(2)

    spread = iota((8, LANES), 0) >> 1
    for half in range(2):
        wait_arrived(lists.at[half, pl.ds(0, LINE - 1)], list_sem.at[half])
        flat = lists.at[half].reshape(64, LANES)
        for t in range(SLOT_ROWS):
            rows = flat[pl.ds(t, 8, stride=8), :]
            for group in range(2):
                codes[1 - half, group, t] = jnp.take_along_axis(
                    rows, spread + 4 * group, axis=0
                )

    odd_row = iota((8, LANES), 0) & 1
    for pair in range(4):
        half = pair & 1
        other = 1 - half
        wait_arrived(got.at[pair, pl.ds(0, 15)], block_sem.at[pair])

        def add_sources(t, carry, pair=pair, half=half):
            for group in range(2):
                code = codes[half, group, t]
                lane = code & (LANES - 1)
                right = (code & LANES) != 0
                bits = (9, 10, 11, 12) if half == 0 else (9, 13, 14, 15)
                signs = [jnp.where((code & (1 << b)) != 0, -1.0, 1.0) for b in bits]

                def total(first, level):
                    if level == 0:
                        table = got[pair, first, group * 8 : group * 8 + 8, :]
                        a = jnp.take_along_axis(table[:, :LANES], lane, axis=1)
                        b = jnp.take_along_axis(table[:, LANES:], lane, axis=1)
                        return jnp.where(right, b, a)
                    upper = total(first + (1 << (level - 1)), level - 1)
                    return total(first, level - 1) + signs[level - 1] * upper

                value = total(0, 4)
                value = jnp.where(((code >> 8) & 1) == odd_row, value, 0.0)
                value = value + pltpu.roll(value, 7, 0)
                for line in range(4):
                    part_sent[pair, group * 4 + line, pl.ds(t, 1), :] = value[
                        2 * line : 2 * line + 1
                    ]
            return carry

        lax.fori_loop(0, SLOT_ROWS, add_sources, 0)

        for line in range(LINE):
            part_sent[pair, line, SLOT_ROWS:, :] = jnp.zeros((1, LANES), jnp.float32)
        for distance in DISTANCES:
            line = on_line(other, distance)
            send(
                part_sent.at[pair, line],
                part_got.at[pair, my_lines[other]],
                2,
                part_sem.at[pair],
                device(other, line, my_core),
            )
        part_got[pair, my_lines[other]] = part_sent[pair, my_lines[other]]

    wait_left(lists.at[:, pl.ds(0, LINE - 1)], 0)
    wait_left(got.at[:, pl.ds(0, 15)], 1)

    own_shard = own_list[...] >> 9
    own_mask = own_used[...]
    for pair in range(4):
        other = 1 - (pair & 1)
        shard_line = (own_shard >> 1 if other == 0 else own_shard >> 4) & 7
        wait_arrived(part_got.at[pair, pl.ds(0, LINE - 1)], part_sem.at[pair])
        total = jnp.zeros((8, LANES), jnp.float32)
        for line in range(LINE):
            value = part_got[pair, line]
            total += jnp.where(parity(shard_line & line) != 0, -value, value)
        picked[my_col, pair // 2, (pair & 1) * 8 : (pair & 1) * 8 + 8, :] = (
            total * own_mask
        )
        if pair & 1:
            for step in (2, 1, 3):
                send(
                    picked.at[my_col, pair // 2],
                    picked.at[my_col, pair // 2],
                    3,
                    picked_sem.at[pair // 2],
                    (me, (my_col + step) & 3),
                )
    wait_left(part_got.at[:, pl.ds(0, LINE - 1)], 2)
    for half in range(2):
        wait_arrived(picked.at[pl.ds(0, 3), half], picked_sem.at[half])
    flat = picked.reshape(COLS * 8, LANES)
    tiles = [flat[pl.ds(t, COLS, stride=8), :] for t in range(SLOT_ROWS)]
    panel_rows = jnp.concatenate(tiles, axis=1)

    row = iota((COLS, LANES), 0)
    lane = iota((COLS, LANES), 1)
    wide = jnp.zeros((COLS, LANES), jnp.float32)
    for j in range(COLS):
        products = tiles[0] * tiles[0][j : j + 1]
        for tile in tiles[1:]:
            products += tile * tile[j : j + 1]
        column = jnp.sum(products, axis=1, keepdims=True)
        wide = jnp.where(lane == (row & 7) * COLS + j, column, wide)
    wide = wide * (1.0 / (SAMPLE_ROWS * LANES))
    grams[me] = jnp.concatenate(
        [
            jnp.sum(wide[:8], axis=0, keepdims=True),
            jnp.sum(wide[8:], axis=0, keepdims=True),
        ],
        axis=0,
    )

    for dy, dz, core in OFFSETS:
        target = on_line(1, dy) * 16 + on_line(0, dz) * 2 + (my_core ^ core)
        send(grams.at[me], grams.at[me], 4, gram_sem.at[0], (target, my_col))
    wait_left(picked.at[pl.ds(0, 3)], 3)
    wait_arrived(grams.at[pl.ds(0, SHARDS - 1)], gram_sem.at[0])
    gram = jnp.sum(grams[...], axis=0)

    rows = jnp.concatenate(
        [jnp.broadcast_to(gram[i : i + 1], (8, LANES)) for i in range(2)], axis=0
    )
    rows = jnp.take_along_axis(rows, ((row & 7) * 16 + lane) & (LANES - 1), axis=1)
    unit = jnp.where(lane - COLS == row, 1.0, 0.0)
    both = jnp.where(lane < COLS, rows, unit)
    for j in range(COLS - 1):
        pivot_row = jnp.broadcast_to(both[j : j + 1], (COLS, LANES))
        pivot = jnp.take_along_axis(pivot_row, jnp.full_like(lane, j), axis=1)
        column = jnp.take_along_axis(both, jnp.full_like(lane, j), axis=1)
        column = jnp.where(row > j, column, 0.0)
        both = both - (column / pivot) * pivot_row
    pivots = jnp.take_along_axis(both, row, axis=1)
    both = both / jnp.sqrt(pivots)
    factor[...] = jnp.where(lane >= row, both, 0.0)[:, :COLS]

    pick_row = iota((8, COLS), 1) == iota((8, COLS), 0) + my_col * WIDTH
    own = jnp.dot(
        pick_row.astype(jnp.float32),
        both[:, COLS : 2 * COLS],
        precision=HIGHEST,
        preferred_element_type=jnp.float32,
    )
    own = jnp.dot(
        own, panel_rows, precision=HIGHEST, preferred_element_type=jnp.float32
    )
    normalized[...] = own[:WIDTH]
    wait_left(grams.at[pl.ds(0, SHARDS - 1)], 4)


def local(panel, signs, samples):
    panel = panel.reshape(WIDTH, 2 * ORDER, LANES).transpose(1, 0, 2)
    panel = panel.reshape(2 * ORDER * WIDTH, LANES)
    signs = signs.reshape(2 * ORDER, LANES)
    samples = samples.reshape(SAMPLE_ROWS, LANES)
    f32, i32, dma = jnp.float32, jnp.int32, pltpu.SemaphoreType.DMA
    factor, normalized = pl.pallas_call(
        kernel,
        out_shape=(
            jax.ShapeDtypeStruct((COLS, COLS), f32),
            jax.ShapeDtypeStruct((WIDTH, CAP), f32),
        ),
        in_specs=[pl.BlockSpec(memory_space=pltpu.HBM)] * 3,
        out_specs=[pl.BlockSpec(memory_space=pltpu.VMEM)] * 2,
        scratch_shapes=[
            pltpu.VMEM((2 * ORDER * WIDTH, LANES), f32),
            pltpu.VMEM((2 * ORDER, LANES), i32),
            pltpu.VMEM((SAMPLE_ROWS, LANES), i32),
            pltpu.VMEM((4, 16, 16, ORDER), f32),
            pltpu.VMEM((4, 16, 16, ORDER), f32),
            pltpu.VMEM((8, LANES), i32),
            pltpu.VMEM((8, LANES), f32),
            pltpu.VMEM((2, LINE, 8, LANES), i32),
            pltpu.VMEM((2, 2, SLOT_ROWS, 8, LANES), i32),
            pltpu.VMEM((4, LINE, 8, LANES), f32),
            pltpu.VMEM((4, LINE, 8, LANES), f32),
            pltpu.VMEM((4, 2, 16, LANES), f32),
            pltpu.VMEM((SHARDS, 2, LANES), f32),
            dma((3,)),
            dma((5,)),
            dma((2,)),
            dma((4,)),
            dma((4,)),
            dma((2,)),
            dma((1,)),
        ],
        compiler_params=pltpu.CompilerParams(
            collective_id=0, has_side_effects=True, vmem_limit_bytes=55100 * 1024
        ),
    )(panel, signs, samples)
    return factor, normalized


def solution(mesh):
    return jax.shard_map(
        local,
        mesh=mesh,
        in_specs=(P("cols", "rows"), P("rows"), P()),
        out_specs=(P(), P("cols", "rows")),
        check_vma=False,
    )
```

time: 629 us -> 51.3 us (0.08)
  blocking collectives: 264 us -> 0 us
  waiting for transfers between devices: 211 us -> 0 us
  local copies, waits for them, and re-layouts: 101 us -> 1.2 us
  Pallas kernels: 0 us -> 49.3 us
  starting transfers between devices: 33.3 us -> 0 us
  other arithmetic: 12.4 us -> 0 us
    psum x1 -> x0, blocking collectives: 254 us -> none  [local(): gram = lax.psum(jnp.dot(everyone, everyone.T, precision=high), 'rows')]
    ppermute x7 -> x0, waiting for transfers between devices: 211 us -> none  [from_partner(): lax.ppermute(shard, axis, [(i, i ^ 1 << bit) for i in range(lax.axis_size...]
    gather x36 -> x0, local copies, waits for them, and re-layouts: 82.2 us -> none  [the longest x34 64 us: local(): upper_edges = jnp.searchsorted(samples, base_rows + block_rows, side='left')]
    pallas_call x0 -> x1, Pallas kernels: none -> 49.3 us  [local(): pl.pallas_call(kernel, out_shape=(jax.ShapeDtypeStruct((COLS, COLS), f32)...]
    ppermute x7 -> x0, starting transfers between devices: 23 us -> none  [from_partner(): lax.ppermute(shard, axis, [(i, i ^ 1 << bit) for i in range(lax.axis_size...]
    all_to_all x1 -> x0, local copies, waits for them, and re-layouts: 15.6 us -> none  [local(): lax.all_to_all(shaped, 'rows', split_axis=1, concat_axis=1, tiled=True)]
    all_to_all x1 -> x0, starting transfers between devices: 10.3 us -> none  [local(): lax.all_to_all(shaped, 'rows', split_axis=1, concat_axis=1, tiled=True)]
    all_gather x1 -> x0, blocking collectives: 9.65 us -> none  [local(): everyone = lax.all_gather(slot_values, 'cols', axis=0, tiled=True)]
  transfers between devices with their start and end apart: 8 -> 0, of which waited for: 7 -> 0; matrix products, arithmetic and copies ran while one was open for 12% -> 0% of each run, Pallas kernels for 0% -> 0%
where the time goes in v2:
time: 51.3 us; the launch traced here: 51.1 us
  Pallas kernels  49.3 us (96%)
  local copies, waits for them, and re-layouts  1.2 us (2%)
  between operations  0.64 us (1%)
    pallas_call x1, Pallas kernels, local(): pl.pallas_call(kernel, out_shape=(jax.ShapeDtypeStruct((COLS, COLS), f32)...  49.3 us
    unnamed x2, local copies, waits for them, and re-layouts  1.2 us

profile of v2, /device:TPU:1, one launch (start us, length us, event | category | flops | bytes accessed | tf_op | source)
XLA Modules:
  0.0 51.1 jit_solution(6362350983951644509)
XLA Ops:
  0.6 49.3 %shard_map.50 = (f32[16,16]{1,0:T(8,128)S(1)}, f32[4,896]{1,0:T(4,128)S(1)}) custom-call(f32[2048,128]{1,0:T(8,128)} %bitcast.7, s32[512,128]{1,0:T(8,128)} %bitcast.8, s32[512,128]{1,0:T(8,128)} %bitcast.9), custom_call_target="tpu_custom_call" | custom-call | tf_op jit(solution)/shard_map/pallas_call | solution.py:417
  49.9 0.6 %copy.8 = f32[16,16]{1,0:T(8,128)} copy(f32[16,16]{1,0:T(8,128)S(1)} %get-tuple-element.4) | data formatting | bytes 2048
  50.5 0.6 %copy.9 = f32[4,896]{1,0:T(4,128)} copy(f32[4,896]{1,0:T(4,128)S(1)} %get-tuple-element.5) | data formatting | bytes 28672

commit v3 on v2

--- a/solution.py
+++ b/solution.py
@@ -21,9 +21,9 @@
 MESH = pl.DeviceIdType.MESH
 HIGHEST = lax.Precision.HIGHEST
 DISTANCES = (4, 3, 5, 2, 6, 1, 7)
-OFFSETS = sorted(
-    ((y, z, c) for y in range(8) for z in range(8) for c in range(2) if y or z or c),
-    key=lambda at: -min(at[0], 8 - at[0]) - min(at[1], 8 - at[1]),
+START_ORDER = sorted(
+    range(SHARDS),
+    key=lambda at: 1.15 * ((at >> 1) & 7) + 0.9 * min(at >> 4, 8 - (at >> 4)),
 )
 
 
@@ -130,6 +130,7 @@
     part_got,
     picked,
     grams,
+    solved,
     local_sem,
     out_sem,
     list_sem,
@@ -351,7 +352,6 @@
         wait_arrived(picked.at[pl.ds(0, 3), half], picked_sem.at[half])
     flat = picked.reshape(COLS * 8, LANES)
     tiles = [flat[pl.ds(t, COLS, stride=8), :] for t in range(SLOT_ROWS)]
-    panel_rows = jnp.concatenate(tiles, axis=1)
 
     row = iota((COLS, LANES), 0)
     lane = iota((COLS, LANES), 1)
@@ -371,9 +371,12 @@
         axis=0,
     )
 
-    for dy, dz, core in OFFSETS:
-        target = on_line(1, dy) * 16 + on_line(0, dz) * 2 + (my_core ^ core)
-        send(grams.at[me], grams.at[me], 4, gram_sem.at[0], (target, my_col))
+    for target in START_ORDER:
+
+        @pl.when(me != target)
+        def _(target=target):
+            send(grams.at[me], grams.at[me], 4, gram_sem.at[0], (target, my_col))
+
     wait_left(picked.at[pl.ds(0, 3)], 3)
     wait_arrived(grams.at[pl.ds(0, SHARDS - 1)], gram_sem.at[0])
     gram = jnp.sum(grams[...], axis=0)
@@ -382,29 +385,27 @@
         [jnp.broadcast_to(gram[i : i + 1], (8, LANES)) for i in range(2)], axis=0
     )
     rows = jnp.take_along_axis(rows, ((row & 7) * 16 + lane) & (LANES - 1), axis=1)
-    unit = jnp.where(lane - COLS == row, 1.0, 0.0)
-    both = jnp.where(lane < COLS, rows, unit)
-    for j in range(COLS - 1):
-        pivot_row = jnp.broadcast_to(both[j : j + 1], (COLS, LANES))
-        pivot = jnp.take_along_axis(pivot_row, jnp.full_like(lane, j), axis=1)
-        column = jnp.take_along_axis(both, jnp.full_like(lane, j), axis=1)
-        column = jnp.where(row > j, column, 0.0)
-        both = both - (column / pivot) * pivot_row
-    pivots = jnp.take_along_axis(both, row, axis=1)
-    both = both / jnp.sqrt(pivots)
-    factor[...] = jnp.where(lane >= row, both, 0.0)[:, :COLS]
-
-    pick_row = iota((8, COLS), 1) == iota((8, COLS), 0) + my_col * WIDTH
-    own = jnp.dot(
-        pick_row.astype(jnp.float32),
-        both[:, COLS : 2 * COLS],
-        precision=HIGHEST,
-        preferred_element_type=jnp.float32,
-    )
-    own = jnp.dot(
-        own, panel_rows, precision=HIGHEST, preferred_element_type=jnp.float32
-    )
-    normalized[...] = own[:WIDTH]
+    columns = [
+        jnp.take_along_axis(rows, jnp.full_like(lane, j), axis=1) for j in range(COLS)
+    ]
+    values = [flat[8 * j : 8 * j + 8, :] for j in range(COLS)]
+    upper = jnp.zeros((COLS, LANES), jnp.float32)
+    roots = jnp.zeros((COLS, LANES), jnp.float32)
+    for j in range(COLS):
+        pivot = columns[j][j : j + 1]
+        share = jnp.where(row > j, columns[j] * (1.0 / pivot), 0.0)
+        for k in range(j + 1, COLS):
+            columns[k] -= share * columns[k][j : j + 1]
+            values[k] -= share[k : k + 1] * values[j]
+        root = 1.0 / jnp.sqrt(pivot)
+        solved[j] = values[j] * root
+        roots = jnp.where(row == j, root, roots)
+        upper = jnp.where((lane == j) & (row <= j), columns[j], upper)
+    factor[...] = (upper * roots)[:, :COLS]
+    for column in range(WIDTH):
+        own = solved[my_col * WIDTH + column]
+        for t in range(SLOT_ROWS):
+            normalized[column : column + 1, t * LANES : (t + 1) * LANES] = own[t : t + 1]
     wait_left(grams.at[pl.ds(0, SHARDS - 1)], 4)
 
 
@@ -436,6 +437,7 @@
             pltpu.VMEM((4, LINE, 8, LANES), f32),
             pltpu.VMEM((4, 2, 16, LANES), f32),
             pltpu.VMEM((SHARDS, 2, LANES), f32),
+            pltpu.VMEM((COLS, 8, LANES), f32),
             dma((3,)),
             dma((5,)),
             dma((2,)),

time: 51.3 us -> 49.6 us (0.967)
  Pallas kernels: 49.3 us -> 47.7 us
    pallas_call x1, Pallas kernels: 49.3 us -> 47.7 us  [local(): pl.pallas_call(kernel, out_shape=(jax.ShapeDtypeStruct((COLS, COLS), f32)...]
where the time goes in v3:
time: 49.6 us; the launch traced here: 49.5 us
  Pallas kernels  47.7 us (96%)
  local copies, waits for them, and re-layouts  1.2 us (2%)
  between operations  0.64 us (1%)
    pallas_call x1, Pallas kernels, local(): pl.pallas_call(kernel, out_shape=(jax.ShapeDtypeStruct((COLS, COLS), f32)...  47.7 us
    unnamed x2, local copies, waits for them, and re-layouts  1.2 us

profile of v3, /device:TPU:1, one launch (start us, length us, event | category | flops | bytes accessed | tf_op | source)
XLA Modules:
  0.0 49.5 jit_solution(17734483644039699066)
XLA Ops:
  0.6 47.7 %shard_map.50 = (f32[16,16]{1,0:T(8,128)S(1)}, f32[4,896]{1,0:T(4,128)S(1)}) custom-call(f32[2048,128]{1,0:T(8,128)} %bitcast.7, s32[512,128]{1,0:T(8,128)} %bitcast.8, s32[512,128]{1,0:T(8,128)} %bitcast.9), custom_call_target="tpu_custom_call" | custom-call | tf_op jit(solution)/shard_map/pallas_call | solution.py:418
  48.3 0.6 %copy.8 = f32[16,16]{1,0:T(8,128)} copy(f32[16,16]{1,0:T(8,128)S(1)} %get-tuple-element.4) | data formatting | bytes 2048
  48.9 0.6 %copy.9 = f32[4,896]{1,0:T(4,128)} copy(f32[4,896]{1,0:T(4,128)S(1)} %get-tuple-element.5) | data formatting | bytes 28672

commit v4 on v3

--- a/solution.py
+++ b/solution.py
@@ -307,7 +307,7 @@
                     ]
             return carry
 
-        lax.fori_loop(0, SLOT_ROWS, add_sources, 0)
+        lax.fori_loop(0, SLOT_ROWS, add_sources, 0, unroll=True)
 
         for line in range(LINE):
             part_sent[pair, line, SLOT_ROWS:, :] = jnp.zeros((1, LANES), jnp.float32)

time: 49.6 us -> 48.9 us (0.986)
  Pallas kernels: 47.7 us -> 46.9 us
    pallas_call x1, Pallas kernels: 47.7 us -> 46.9 us  [local(): pl.pallas_call(kernel, out_shape=(jax.ShapeDtypeStruct((COLS, COLS), f32)...]
where the time goes in v4:
time: 48.9 us; the launch traced here: 48.7 us
  Pallas kernels  46.9 us (96%)
  local copies, waits for them, and re-layouts  1.2 us (2%)
  between operations  0.64 us (1%)
    pallas_call x1, Pallas kernels, local(): pl.pallas_call(kernel, out_shape=(jax.ShapeDtypeStruct((COLS, COLS), f32)...  46.9 us
    unnamed x2, local copies, waits for them, and re-layouts  1.2 us

profile of v4, /device:TPU:1, one launch (start us, length us, event | category | flops | bytes accessed | tf_op | source)
XLA Modules:
  0.0 48.7 jit_solution(13517154996953657018)
XLA Ops:
  0.6 46.9 %shard_map.50 = (f32[16,16]{1,0:T(8,128)S(1)}, f32[4,896]{1,0:T(4,128)S(1)}) custom-call(f32[2048,128]{1,0:T(8,128)} %bitcast.7, s32[512,128]{1,0:T(8,128)} %bitcast.8, s32[512,128]{1,0:T(8,128)} %bitcast.9), custom_call_target="tpu_custom_call" | custom-call | tf_op jit(solution)/shard_map/pallas_call | solution.py:418
  47.5 0.6 %copy.8 = f32[16,16]{1,0:T(8,128)} copy(f32[16,16]{1,0:T(8,128)S(1)} %get-tuple-element.4) | data formatting | bytes 2048
  48.1 0.6 %copy.9 = f32[4,896]{1,0:T(4,128)} copy(f32[4,896]{1,0:T(4,128)S(1)} %get-tuple-element.5) | data formatting | bytes 28672

commit v5 on v4

--- a/solution.py
+++ b/solution.py
@@ -170,6 +170,19 @@
     def wait_left(like, out):
         pltpu.make_async_copy(like, like, out_sem.at[out]).wait()
 
+    barrier = pltpu.get_barrier_semaphore()
+
+    def greet(target):
+        pl.semaphore_signal(barrier, inc=1, device_id=target, device_id_type=MESH)
+
+    for distance in DISTANCES:
+        for half in range(2):
+            for flip in range(2):
+                greet(device(half, on_line(half, distance), my_core ^ flip))
+    for step in range(1, 4):
+        greet((me, (my_col + step) & 3))
+    greet(device(0, my_z, 1 - my_core))
+
     loads = [
         pltpu.make_async_copy(panel, panel_v, local_sem.at[2]),
         pltpu.make_async_copy(signs, signs_v, local_sem.at[1]),
@@ -177,19 +190,6 @@
     ]
     for load in loads:
         load.start()
-
-    barrier = pltpu.get_barrier_semaphore()
-
-    def greet(target):
-        pl.semaphore_signal(barrier, inc=1, device_id=target, device_id_type=MESH)
-
-    for distance in DISTANCES:
-        for half in range(2):
-            for flip in range(2):
-                greet(device(half, on_line(half, distance), my_core ^ flip))
-    for step in range(1, 4):
-        greet((me, (my_col + step) & 3))
-    greet(device(0, my_z, 1 - my_core))
 
     inner = hadamard_rows(iota((ORDER, ORDER), 0))
     outer = []
@@ -218,29 +218,32 @@
         sent[pair] = values.reshape(16, 16, ORDER)
         got[pair, my_sources[half]] = sent[pair, my_sources[half]]
 
-    def send_block(pair, half, line, core):
+    def send_block(pair, half, line, core, rows, arrived):
         send(
-            sent.at[pair, line * 2 + core],
-            got.at[pair, my_sources[half]],
+            sent.at[pair, line * 2 + core, rows],
+            got.at[pair, my_sources[half], rows],
             1,
-            block_sem.at[pair],
+            block_sem.at[arrived],
             device(half, line, core),
         )
 
-    def send_blocks(first):
+    def send_blocks(first, rows, arrived):
         for distance in DISTANCES:
             for half in range(2):
                 for flip in range(2):
+                    line = on_line(half, distance)
                     send_block(
-                        first + half, half, on_line(half, distance), my_core ^ flip
+                        first + half, half, line, my_core ^ flip, rows, arrived + half
                     )
         for half in range(2):
-            send_block(first + half, half, my_lines[half], 1 - my_core)
+            send_block(
+                first + half, half, my_lines[half], 1 - my_core, rows, arrived + half
+            )
 
     transform(0)
     transform(1)
     pl.semaphore_wait(barrier, 32)
-    send_blocks(0)
+    send_blocks(0, pl.ds(0, 16), 0)
     transform(2)
     transform(3)
 
@@ -262,7 +265,8 @@
                 list_sem.at[half],
                 device(half, line, my_core),
             )
-    send_blocks(2)
+    for group in range(2):
+        send_blocks(2, pl.ds(8 * group, 8), 2 + 2 * group)
 
     spread = iota((8, LANES), 0) >> 1
     for half in range(2):
@@ -276,13 +280,11 @@
                 )
 
     odd_row = iota((8, LANES), 0) & 1
-    for pair in range(4):
+    def sample(pair, groups):
         half = pair & 1
-        other = 1 - half
-        wait_arrived(got.at[pair, pl.ds(0, 15)], block_sem.at[pair])
-
-        def add_sources(t, carry, pair=pair, half=half):
-            for group in range(2):
+
+        def add_sources(t, carry):
+            for group in groups:
                 code = codes[half, group, t]
                 lane = code & (LANES - 1)
                 right = (code & LANES) != 0
@@ -308,18 +310,44 @@
             return carry
 
         lax.fori_loop(0, SLOT_ROWS, add_sources, 0, unroll=True)
-
-        for line in range(LINE):
-            part_sent[pair, line, SLOT_ROWS:, :] = jnp.zeros((1, LANES), jnp.float32)
+        for group in groups:
+            for line in range(4 * group, 4 * group + 4):
+                part_sent[pair, line, SLOT_ROWS:, :] = jnp.zeros(
+                    (1, LANES), jnp.float32
+                )
+
+    def send_sums(pair, line):
+        other = 1 - (pair & 1)
+        send(
+            part_sent.at[pair, line],
+            part_got.at[pair, my_lines[other]],
+            2,
+            part_sem.at[pair],
+            device(other, line, my_core),
+        )
+
+    for pair in range(2):
+        other = 1 - pair
+        wait_arrived(got.at[pair, pl.ds(0, 15)], block_sem.at[pair])
+        sample(pair, (0, 1))
         for distance in DISTANCES:
-            line = on_line(other, distance)
-            send(
-                part_sent.at[pair, line],
-                part_got.at[pair, my_lines[other]],
-                2,
-                part_sem.at[pair],
-                device(other, line, my_core),
+            send_sums(pair, on_line(other, distance))
+        part_got[pair, my_lines[other]] = part_sent[pair, my_lines[other]]
+    for group in range(2):
+        for pair in range(2, 4):
+            other = 1 - (pair & 1)
+            wait_arrived(
+                got.at[pair, pl.ds(0, 15), pl.ds(0, 8)], block_sem.at[pair + 2 * group]
             )
+            sample(pair, (group,))
+            for line in range(4 * group, 4 * group + 4):
+
+                @pl.when(line != my_lines[other])
+                def _(pair=pair, line=line):
+                    send_sums(pair, line)
+
+    for pair in range(2, 4):
+        other = 1 - (pair & 1)
         part_got[pair, my_lines[other]] = part_sent[pair, my_lines[other]]
 
     wait_left(lists.at[:, pl.ds(0, LINE - 1)], 0)
@@ -441,7 +469,7 @@
             dma((3,)),
             dma((5,)),
             dma((2,)),
-            dma((4,)),
+            dma((6,)),
             dma((4,)),
             dma((2,)),
             dma((1,)),

time: 48.9 us -> 48.4 us (0.990)
  Pallas kernels: 46.9 us -> 46.4 us
    pallas_call x1, Pallas kernels: 46.9 us -> 46.4 us  [local(): pl.pallas_call(kernel, out_shape=(jax.ShapeDtypeStruct((COLS, COLS), f32)...]
where the time goes in v5:
time: 48.4 us; the launch traced here: 48.2 us
  Pallas kernels  46.4 us (96%)
  local copies, waits for them, and re-layouts  1.2 us (2%)
  between operations  0.64 us (1%)
    pallas_call x1, Pallas kernels, local(): pl.pallas_call(kernel, out_shape=(jax.ShapeDtypeStruct((COLS, COLS), f32)...  46.4 us
    unnamed x2, local copies, waits for them, and re-layouts  1.2 us

profile of v5, /device:TPU:1, one launch (start us, length us, event | category | flops | bytes accessed | tf_op | source)
XLA Modules:
  0.0 48.2 jit_solution(15094361337995662817)
XLA Ops:
  0.6 46.4 %shard_map.50 = (f32[16,16]{1,0:T(8,128)S(1)}, f32[4,896]{1,0:T(4,128)S(1)}) custom-call(f32[2048,128]{1,0:T(8,128)} %bitcast.7, s32[512,128]{1,0:T(8,128)} %bitcast.8, s32[512,128]{1,0:T(8,128)} %bitcast.9), custom_call_target="tpu_custom_call" | custom-call | tf_op jit(solution)/shard_map/pallas_call | solution.py:446
  47.0 0.6 %copy.8 = f32[16,16]{1,0:T(8,128)} copy(f32[16,16]{1,0:T(8,128)S(1)} %get-tuple-element.4) | data formatting | bytes 2048
  47.6 0.6 %copy.9 = f32[4,896]{1,0:T(4,128)} copy(f32[4,896]{1,0:T(4,128)S(1)} %get-tuple-element.5) | data formatting | bytes 28672

commit v6 on v5

--- a/solution.py
+++ b/solution.py
@@ -276,10 +276,13 @@
             rows = flat[pl.ds(t, 8, stride=8), :]
             for group in range(2):
                 codes[1 - half, group, t] = jnp.take_along_axis(
-                    rows, spread + 4 * group, axis=0
-                )
+                    rows, spread + 4 * group, axis=0, mode="promise_in_bounds")
 
     odd_row = iota((8, LANES), 0) & 1
+    for pair in range(4):
+        for line in range(LINE):
+            part_sent[pair, line, SLOT_ROWS:, :] = jnp.zeros((1, LANES), jnp.float32)
+
     def sample(pair, groups):
         half = pair & 1
 
@@ -294,8 +297,8 @@
                 def total(first, level):
                     if level == 0:
                         table = got[pair, first, group * 8 : group * 8 + 8, :]
-                        a = jnp.take_along_axis(table[:, :LANES], lane, axis=1)
-                        b = jnp.take_along_axis(table[:, LANES:], lane, axis=1)
+                        a = jnp.take_along_axis(table[:, :LANES], lane, axis=1, mode="promise_in_bounds")
+                        b = jnp.take_along_axis(table[:, LANES:], lane, axis=1, mode="promise_in_bounds")
                         return jnp.where(right, b, a)
                     upper = total(first + (1 << (level - 1)), level - 1)
                     return total(first, level - 1) + signs[level - 1] * upper
@@ -310,11 +313,6 @@
             return carry
 
         lax.fori_loop(0, SLOT_ROWS, add_sources, 0, unroll=True)
-        for group in groups:
-            for line in range(4 * group, 4 * group + 4):
-                part_sent[pair, line, SLOT_ROWS:, :] = jnp.zeros(
-                    (1, LANES), jnp.float32
-                )
 
     def send_sums(pair, line):
         other = 1 - (pair & 1)
@@ -359,10 +357,11 @@
         other = 1 - (pair & 1)
         shard_line = (own_shard >> 1 if other == 0 else own_shard >> 4) & 7
         wait_arrived(part_got.at[pair, pl.ds(0, LINE - 1)], part_sem.at[pair])
-        total = jnp.zeros((8, LANES), jnp.float32)
-        for line in range(LINE):
-            value = part_got[pair, line]
-            total += jnp.where(parity(shard_line & line) != 0, -value, value)
+        signs = [jnp.where((shard_line & (1 << b)) != 0, -1.0, 1.0) for b in range(3)]
+        parts = [part_got[pair, line] for line in range(LINE)]
+        for sign in signs:
+            parts = [a + sign * b for a, b in zip(parts[::2], parts[1::2])]
+        total = parts[0]
         picked[my_col, pair // 2, (pair & 1) * 8 : (pair & 1) * 8 + 8, :] = (
             total * own_mask
         )
@@ -414,7 +413,7 @@
     )
     rows = jnp.take_along_axis(rows, ((row & 7) * 16 + lane) & (LANES - 1), axis=1)
     columns = [
-        jnp.take_along_axis(rows, jnp.full_like(lane, j), axis=1) for j in range(COLS)
+        jnp.take_along_axis(rows, jnp.full_like(lane, j), axis=1, mode="promise_in_bounds") for j in range(COLS)
     ]
     values = [flat[8 * j : 8 * j + 8, :] for j in range(COLS)]
     upper = jnp.zeros((COLS, LANES), jnp.float32)

time: 48.4 us -> 48.4 us (level)
  no operation moved by 1% of the time
where the time goes in v6:
time: 48.4 us; the launch traced here: 48.2 us
  Pallas kernels  46.4 us (96%)
  local copies, waits for them, and re-layouts  1.2 us (2%)
  between operations  0.64 us (1%)
    pallas_call x1, Pallas kernels, local(): pl.pallas_call(kernel, out_shape=(jax.ShapeDtypeStruct((COLS, COLS), f32)...  46.4 us
    unnamed x2, local copies, waits for them, and re-layouts  1.2 us

profile of v6, /device:TPU:1, one launch (start us, length us, event | category | flops | bytes accessed | tf_op | source)
XLA Modules:
  0.0 48.2 jit_solution(4278894919517463802)
XLA Ops:
  0.6 46.4 %shard_map.50 = (f32[16,16]{1,0:T(8,128)S(1)}, f32[4,896]{1,0:T(4,128)S(1)}) custom-call(f32[2048,128]{1,0:T(8,128)} %bitcast.7, s32[512,128]{1,0:T(8,128)} %bitcast.8, s32[512,128]{1,0:T(8,128)} %bitcast.9), custom_call_target="tpu_custom_call" | custom-call | tf_op jit(solution)/shard_map/pallas_call | solution.py:445
  47.0 0.6 %copy.8 = f32[16,16]{1,0:T(8,128)} copy(f32[16,16]{1,0:T(8,128)S(1)} %get-tuple-element.4) | data formatting | bytes 2048
  47.6 0.6 %copy.9 = f32[4,896]{1,0:T(4,128)} copy(f32[4,896]{1,0:T(4,128)S(1)} %get-tuple-element.5) | data formatting | bytes 28672
